TPU v7x, 32 devices: a whole 2x2x4 slice. The times are simulated.
32 devices in a mesh: leaf: 4 (over y, x), sep: 4 (over z), mode: 2 (over core).
Axes of the slice: x: 2, y: 2, z: 4, core: 2. Of those that a mesh axis runs over, the one named last changes fastest.
Arguments:
- modes: bfloat16 [128, 2048, 256], P(('leaf', 'sep'), 'mode'), may hold values from -0.125 to 0.125
- coupling: bfloat16 [128, 2048, 256], P(('leaf', 'sep'), 'mode'), may hold values from -6 to 6
- eigenvalues: float32 [128, 256], P(('leaf', 'sep'), 'mode'), may hold values from 200 to 4000
- separator_of: int32 [128, 1], P(('leaf', 'sep')), may hold values from 0 to 3; in each aligned block of 8 rows (0 to 7, 8 to 15, ...) at most 2 rows name the same one
- row_offset: int32 [128], P(('leaf', 'sep')), may hold values from 0 to 256
- stiffness: bfloat16 [4, 512, 512], P('sep', None, ('leaf', 'mode')), may hold values from -1 to 40
- start_block: bfloat16 [4, 512, 256], P('sep', ('leaf', 'mode')), may hold values from -40 to 40
- rotations: bfloat16 [4, 2, 256, 256], P('sep'), may hold values from -0.375 to 0.375
Outputs:
- subspace: bfloat16 [4, 512, 256], P('sep', ('leaf', 'mode'))
- column_norms: float32 [4, 2, 256], P('sep')
Inputs may be any that keep to these rules, and one draw needn't show every extreme that they name: `separator_of`: among the 8 leaves of one device at most 2 couple to one separator, and in every draw some separator gets exactly 2 of them.
All inputs are finite; a program needn't handle non-finite values.
Results may differ from a plain program's by a relative error of at most 0.0075.
Values may be sent and summed in bfloat16 or wider, within the bound.
A program may use at most 64 MiB of HBM per device.

v0:
```python
import jax
import jax.numpy as jnp
from jax import lax
from jax.sharding import PartitionSpec as P

SEP_ROWS = 512
CAP = 2
ITERS = 2


epsilon = 1e-06


def leaf_projection(modes, coupling, eigenvalues):
    summed = lax.psum_scatter(
        jnp.einsum("ldm,ldw->mlw", modes, coupling, preferred_element_type=jnp.float32),
        "mode",
        scatter_dimension=0,
        tiled=True,
    )
    return (summed / jnp.sqrt(eigenvalues.T)[:, :, None]).astype(jnp.bfloat16)


def route_blocks(scaled, separator_of, row_offset):
    groups = lax.axis_size("sep")
    leaves = scaled.shape[1]
    target = separator_of[:, 0]
    leaf_order = jnp.arange(leaves)
    earlier = (target[:, None] == target[None, :]) & (leaf_order[None, :] < leaf_order[:, None])
    position = jnp.sum(earlier.astype(jnp.int32), 1)
    slot_of = target * CAP + position
    slot_table = slot_of[None, :] == jnp.arange(groups * CAP)[:, None]
    send_blocks = jnp.einsum(
        "sl,mlw->smw", slot_table.astype(jnp.bfloat16), scaled, preferred_element_type=jnp.float32
    ).astype(jnp.bfloat16)
    send_offsets = jnp.sum(jnp.where(slot_table, row_offset[None, :], 0), 1)
    block_shape = (groups, CAP, send_blocks.shape[1], send_blocks.shape[2])
    got_blocks, got_offsets = (
        lax.all_to_all(
            send_blocks.reshape(block_shape), "sep", split_axis=0, concat_axis=0, tiled=True
        ),
        lax.all_to_all(
            send_offsets.reshape(groups, CAP), "sep", split_axis=0, concat_axis=0, tiled=True
        ),
    )
    return (
        got_blocks.reshape(groups * CAP, block_shape[2], block_shape[3]),
        got_offsets.reshape(groups * CAP),
    )


def coupled_correction(full_block, blocks, offsets):
    width_rows = blocks.shape[2]

    def add_slot(slot_index, accumulated):
        offset = offsets[slot_index]
        weights = blocks[slot_index]
        window = lax.dynamic_slice_in_dim(full_block, offset, width_rows, 0)
        projected = jnp.dot(weights, window, preferred_element_type=jnp.float32).astype(
            jnp.bfloat16
        )
        update = jnp.einsum("mw,mc->wc", weights, projected, preferred_element_type=jnp.float32)
        current = lax.dynamic_slice_in_dim(accumulated, offset, width_rows, 0)
        return lax.dynamic_update_slice_in_dim(accumulated, current + update, offset, 0)

    initial = jnp.zeros(full_block.shape, jnp.float32)
    return lax.fori_loop(0, blocks.shape[0], add_slot, initial)


def gather_rows(own_block):
    return lax.all_gather(own_block, ("leaf", "mode"), axis=0, tiled=True)


def per_device(
    modes, coupling, eigenvalues, separator_of, row_offset, stiffness, start_block, rotations
):
    scaled = leaf_projection(modes, coupling, eigenvalues)
    blocks, offsets = route_blocks(scaled, separator_of, row_offset)
    stiff_columns = stiffness[0]
    own_block = start_block[0]
    ritz_turns = rotations[0]
    own_rows = own_block.shape[0]
    norm_list = []
    for iteration in range(ITERS):
        full_block = gather_rows(own_block)
        correction = coupled_correction(full_block, blocks, offsets)

        def assemble_rows(first_row, row_count, block_now=own_block, correction_now=correction):
            product = jnp.dot(stiff_columns, block_now, preferred_element_type=jnp.float32)
            return product - correction_now

        summed = lax.psum_scatter(
            assemble_rows(jnp.int32(0), lax.axis_size(("leaf", "mode")) * own_rows),
            ("leaf", "mode"),
            scatter_dimension=0,
            tiled=True,
        )
        squares = lax.psum(jnp.sum(summed * summed, 0), ("leaf", "mode"))
        column_scale = jnp.sqrt(squares / SEP_ROWS + epsilon)
        normed = (summed / column_scale).astype(jnp.bfloat16)
        own_block = jnp.dot(
            normed, ritz_turns[iteration], preferred_element_type=jnp.float32
        ).astype(jnp.bfloat16)
        norm_list.append(column_scale)
    return (own_block[None], jnp.stack(norm_list)[None])


def solution(mesh):
    in_specs = (
        P(("leaf", "sep"), "mode", None),
        P(("leaf", "sep"), "mode", None),
        P(("leaf", "sep"), "mode"),
        P(("leaf", "sep"), None),
        P(("leaf", "sep")),
        P("sep", None, ("leaf", "mode")),
        P("sep", ("leaf", "mode"), None),
        P("sep", None, None, None),
    )
    out_specs = (P("sep", ("leaf", "mode"), None), P("sep", None, None))
    return jax.shard_map(
        per_device, mesh=mesh, in_specs=in_specs, out_specs=out_specs, check_vma=False
    )
```

profile of v0, /device:TPU:0, one launch (start us, length us, event | category | flops | bytes accessed | tf_op | source)
XLA Modules:
  0.0 241.5 jit_solution(9855624408712388159)
XLA Ops:
  7.3 6.2 %convolution_bitcast_fusion = f32[256,8,256]{0,2,1:T(8,128)} fusion(bf16[8,1024,256]{2,1,0:T(8,128)(2,1)} %param.13, bf16[8,1024,256]{2,1,0:T(8,128)(2,1)} %param.12), kind=kOutput, calls=%fused_computation.13 | convolution fusion | flops 1073741824 | bytes 10485760 | tf_op jit(solution)/shard_map/ldm,ldw->mlw/dot_general | solution.py:16
  14.5 6.3 %all-to-all-start = ((s32[4,1,2]{2,1,0:T(1,128)}), s32[4,1,2]{2,1,0:T(1,128)S(1)}, u32[]{:S(2)}, u32[]{:S(2)}) async-start(s32[4,1,2]{2,1,0:T(1,128)} %bitcast.7), calls=%async_computation | async-start | bytes 4096 | tf_op jit(solution)/shard_map/all_to_all | solution.py:42
  20.8 5.1 %reduce-scatter.6.cloned.1.call-done = f32[128,8,256]{0,2,1:T(8,128)} async-done(((f32[256,8,256]{0,2,1:T(8,128)}), f32[128,8,256]{0,2,1:T(8,128)}) %reduce-scatter.6.cloned.1.call-update) | async-done | bytes 1048592 | tf_op jit(solution)/shard_map/reduce_scatter | solution.py:15
  29.3 4.9 %all-to-all-start.1 = ((bf16[4,2,128,256]{3,1,2,0:T(2,128)(2,1)}), bf16[4,2,128,256]{3,1,2,0:T(2,128)(2,1)S(1)}, u32[]{:S(2)}, u32[]{:S(2)}) async-start(bf16[4,2,128,256]{3,1,2,0:T(2,128)(2,1)} %copy.30), calls=%async_computation.2 | async-start | bytes 1048576 | tf_op jit(solution)/shard_map/all_to_all | solution.py:39
  34.2 9.3 %all-gather = bf16[1,512,256]{2,1,0:T(8,128)(2,1)S(1)} all-gather(bf16[1,64,256]{2,1,0:T(8,128)(2,1)S(1)} %copy-done.1), channel_id=2, replica_groups=mesh['leaf'=4,'sep'=4,'mode'=2] {'leaf','mode'}, dimensions={1}, use_global_device_ids=true | all-gather | bytes 294912 | tf_op jit(solution)/shard_map/all_gather | solution.py:71
  44.7 4.4 %all-to-all-done.1 = bf16[4,2,128,256]{3,1,2,0:T(2,128)(2,1)S(1)} async-done(((bf16[4,2,128,256]{3,1,2,0:T(2,128)(2,1)}), bf16[4,2,128,256]{3,1,2,0:T(2,128)(2,1)S(1)}, u32[]{:S(2)}, u32[]{:S(2)}) %all-to-all-start.1) | async-done | bytes 524320 | tf_op jit(solution)/shard_map/all_to_all | solution.py:39
  49.3 34.8 %while.26 = (s32[]{:T(128)}, f32[512,256]{1,0:T(8,128)S(1)}, s32[8]{0:T(128)S(1)}, bf16[8,128,256]{2,1,0:T(8,128)(2,1)S(1)}, bf16[512,256]{1,0:T(8,128)(2,1)S(1)}, /*index=5*/s32[]{:T(128)}, s32[]{:T(128)}, s32[]{:T(128)}) while((s32[]{:T(128)}, f32[512,256]{1,0:T(8,128)S(1)}, s32[8]{0:T(128)S(1)}, bf16[8,128,256]{2,1,0:T(8,128)(2,1)S(1)}, ...), condition=%wide.region_4.5_spmd, body=%wide.region_3.4_spmd.sunk | while | flops 33652740 | bytes 1312903 | solution.py:67
  64.6 1.6 dynamic_update_slice.16
  73.2 1.9 dynamic_update_slice.16
  78.0 1.6 dynamic_update_slice.16
  82.5 1.5 dynamic_update_slice.16
  85.2 33.3 %reduce-scatter.8.cloned.1.call-done = f32[64,256]{1,0:T(8,128)} async-done(((f32[512,256]{1,0:T(8,128)}), f32[64,256]{1,0:T(8,128)}) %reduce-scatter.8.cloned.1.call-update) | async-done | bytes 65552 | tf_op jit(solution)/shard_map/reduce_scatter | solution.py:92
  119.4 12.2 %psum.14 = f32[256]{0:T(256)S(1)} all-reduce(f32[256]{0:T(256)S(1)} %multiply_reduce_fusion.1), channel_id=1, replica_groups=mesh['leaf'=4,'sep'=4,'mode'=2] {'leaf','mode'}, use_global_device_ids=true, to_apply=%region_7.8 | all-reduce | flops 256 | bytes 2048 | tf_op jit(solution)/shard_map/psum | solution.py:98
  132.6 9.2 %all_gather.7 = bf16[512,256]{1,0:T(8,128)(2,1)S(1)} all-gather(bf16[64,256]{1,0:T(8,128)(2,1)S(1)} %convolution_convert_fusion.4), channel_id=1, replica_groups=mesh['leaf'=4,'sep'=4,'mode'=2] {'leaf','mode'}, dimensions={0}, use_global_device_ids=true | all-gather | bytes 294912 | tf_op jit(solution)/shard_map/all_gather | solution.py:71
  141.8 42.4 %while.27 = (s32[]{:T(128)}, f32[512,256]{0,1:T(8,128)S(1)}, s32[8]{0:T(128)S(1)}, bf16[8,128,256]{2,1,0:T(8,128)(2,1)S(1)}, bf16[512,256]{1,0:T(8,128)(2,1)S(1)}, /*index=5*/s32[]{:T(128)}, s32[]{:T(128)}, s32[]{:T(128)}) while((s32[]{:T(128)}, f32[512,256]{0,1:T(8,128)S(1)}, s32[8]{0:T(128)S(1)}, bf16[8,128,256]{2,1,0:T(8,128)(2,1)S(1)}, ...), condition=%wide.region_9.10_spmd, body=%wide.region_8.9_spmd.sunk | while | flops 33652740 | bytes 2884751 | solution.py:67
  145.2 1.8 dynamic_update_slice.17
  150.4 1.8 dynamic_update_slice.17
  155.6 1.8 dynamic_update_slice.17
  160.8 2.2 dynamic_update_slice.17
  170.8 2.2 dynamic_update_slice.17
  176.4 2.2 dynamic_update_slice.17
  182.0 2.2 dynamic_update_slice.17
  185.5 34.7 %reduce-scatter.10.cloned.1.call-done = f32[64,256]{1,0:T(8,128)} async-done(((f32[512,256]{1,0:T(8,128)}), f32[64,256]{1,0:T(8,128)}) %reduce-scatter.10.cloned.1.call-update) | async-done | bytes 65552
  221.3 12.2 %psum.15 = f32[256]{0:T(256)S(1)} all-reduce(f32[256]{0:T(256)S(1)} %multiply_reduce_fusion), channel_id=1, replica_groups=mesh['leaf'=4,'sep'=4,'mode'=2] {'leaf','mode'}, use_global_device_ids=true, to_apply=%region_12.13 | all-reduce | flops 256 | bytes 2048 | tf_op jit(solution)/shard_map/psum | solution.py:98
  (107 shorter events, 36.8 us)
Async XLA Ops:
  7.2 76.9 %copy-start = (bf16[1,512,64]{1,2,0:T(8,128)(2,1)S(1)}, bf16[1,512,64]{1,2,0:T(8,128)(2,1)}, u32[]{:S(2)}) copy-start(bf16[1,512,64]{1,2,0:T(8,128)(2,1)} %param.17) | copy-start | bytes 196612
  7.2 6.3 %copy-start.4 = (s32[8,1]{0,1:T(1,128)S(1)}, s32[8,1]{0,1:T(1,128)}, u32[]{:S(2)}) copy-start(s32[8,1]{0,1:T(1,128)} %param.15) | copy-start | bytes 100
  7.2 6.5 %copy-start.5 = (s32[8]{0:T(128)S(1)}, s32[8]{0:T(128)}, u32[]{:S(2)}) copy-start(s32[8]{0:T(128)} %param.16) | copy-start | bytes 100
  7.2 13.6 %copy-start.2 = (f32[8,128]{1,0:T(8,128)S(1)}, f32[8,128]{1,0:T(8,128)}, u32[]{:S(2)}) copy-start(f32[8,128]{1,0:T(8,128)} %param.14) | copy-start | bytes 12292
  7.2 18.8 %reduce-scatter.6.cloned.1.call-start = ((), (), s32[]{:S(2)}) async-start(), calls=%async_computation.5 | async-start | bytes 3145728 | tf_op jit(solution)/shard_map/reduce_scatter | solution.py:15
  13.5 20.7 %copy-start.1 = (bf16[1,64,256]{2,1,0:T(8,128)(2,1)S(1)}, bf16[1,64,256]{2,1,0:T(8,128)(2,1)}, u32[]{:S(2)}) copy-start(bf16[1,64,256]{2,1,0:T(8,128)(2,1)} %param.18) | copy-start | bytes 98308
  14.5 14.8 %all-to-all-start = ((s32[4,1,2]{2,1,0:T(1,128)}), s32[4,1,2]{2,1,0:T(1,128)S(1)}, u32[]{:S(2)}, u32[]{:S(2)}) async-start(s32[4,1,2]{2,1,0:T(1,128)} %bitcast.7), calls=%async_computation | async-start | bytes 4096 | tf_op jit(solution)/shard_map/all_to_all | solution.py:42
  29.3 19.8 %all-to-all-start.1 = ((bf16[4,2,128,256]{3,1,2,0:T(2,128)(2,1)}), bf16[4,2,128,256]{3,1,2,0:T(2,128)(2,1)S(1)}, u32[]{:S(2)}, u32[]{:S(2)}) async-start(bf16[4,2,128,256]{3,1,2,0:T(2,128)(2,1)} %copy.30), calls=%async_computation.2 | async-start | bytes 1048576 | tf_op jit(solution)/shard_map/all_to_all | solution.py:39
  34.2 84.3 %reduce-scatter.8.cloned.1.call-start = ((), (), s32[]{:S(2)}) async-start(), calls=%async_computation.6 | async-start | bytes 589824 | tf_op jit(solution)/shard_map/reduce_scatter | solution.py:92
  49.3 82.3 %copy-start.3 = (bf16[1,2,256,256]{3,2,1,0:T(8,128)(2,1)S(1)}, bf16[1,2,256,256]{3,2,1,0:T(8,128)(2,1)}, u32[]{:S(2)}) copy-start(bf16[1,2,256,256]{3,2,1,0:T(8,128)(2,1)} %param.19) | copy-start | bytes 786436
  85.1 135.1 %reduce-scatter.10.cloned.1.call-start = ((), (), s32[]{:S(2)}) async-start(), calls=%async_computation.7 | async-start | bytes 589824
Sparse Core Ops, SparseCore 0:
  13.6 12.2 reduce-scatter.5
  85.3 33.1 reduce-scatter.7
  185.6 34.5 reduce-scatter.9
where the time goes:
time: 243 us; the launch traced here: 242 us
  waiting for transfers between devices  77.6 us (32%)
  local copies, waits for them, and re-layouts  44.6 us (18%)
  blocking collectives  42.9 us (18%)
  loops' own time  31.8 us (13%)
  matrix products  15.6 us (6%)
  between operations  13.9 us (6%)
  starting transfers between devices  11.3 us (5%)
  other arithmetic  3.86 us (2%)
    unnamed x4, waiting for transfers between devices  34.8 us
    reduce_scatter x1, waiting for transfers between devices, per_device(): lax.psum_scatter(assemble_rows(jnp.int32(0), lax.axis_size(('leaf', 'mode...  33.3 us
    another operation x2, loops' own time, coupled_correction(): return lax.fori_loop(0, blocks.shape[0], add_slot, initial)  31.8 us
    dynamic_update_slice x24, local copies, waits for them, and re-layouts, add_slot(): lax.dynamic_update_slice_in_dim(accumulated, current + update, offset, 0)  27.9 us
    psum x2, blocking collectives, per_device(): squares = lax.psum(jnp.sum(summed * summed, 0), ('leaf', 'mode'))  24.4 us
    all_gather x2, blocking collectives, gather_rows(): return lax.all_gather(own_block, ('leaf', 'mode'), axis=0, tiled=True)  18.5 us
    dynamic_slice x16, local copies, waits for them, and re-layouts, add_slot(): offset = offsets[slot_index]  9.38 us
    all_to_all x1, starting transfers between devices, route_blocks(): lax.all_to_all(send_offsets.reshape(groups, CAP), 'sep', split_axis=0, co...  6.32 us
  transfers between devices with their start and end apart: 5, of which 4 were waited for; matrix products, arithmetic and copies ran while one was open for 2% of the time, Pallas kernels for 0%

commit v1 on v0

v1 whole, which is shorter than its diff:
```python
import functools

import jax
import jax.numpy as jnp
from jax import lax
from jax.experimental import pallas as pl
from jax.experimental.pallas import tpu as pltpu
from jax.sharding import PartitionSpec as P

CAP = 2
EPSILON = 1e-06
MESH = pl.DeviceIdType.MESH
F32 = jnp.float32
BF16 = jnp.bfloat16


def remote(src, dst, send_sem, recv_sem, **device):
    return pltpu.make_async_remote_copy(
        src_ref=src,
        dst_ref=dst,
        send_sem=send_sem,
        recv_sem=recv_sem,
        device_id=device,
        device_id_type=MESH,
    )


def contract(a, b, dim_a, dim_b):
    return lax.dot_general(a, b, (((dim_a,), (dim_b,)), ((), ())), preferred_element_type=F32)


def kernel(
    nl, ns,
    separator_of, row_offset, modes_hbm, coupling_hbm, eigenvalues, stiffness, start_block, rotations,
    out, norms,
    modes, coupling, part_own, part_send, part_recv, scaled,
    slot_send, slot_recv, offset_send, offset_recv, padded,
    gram, gram_send, gram_recv, leaf_own, leaf_send, leaf_recv, operator, block, normed_rows,
    hbm_sem, part_ssem, part_rsem, block_ssem, block_rsem, slot_ssem, slot_rsem,
    offset_ssem, offset_rsem, leaf_ssem, leaf_rsem, oper_ssem, oper_rsem, core_ssem, core_rsem,
):
    leaf, sep, core = lax.axis_index("leaf"), lax.axis_index("sep"), lax.axis_index("mode")
    other = 1 - core
    leaves, _, half = scaled.shape
    iface = scaled.shape[1]
    rows = padded.shape[0]
    cols = out.shape[2]

    loads = []
    for l in range(leaves):
        pair = (
            pltpu.make_async_copy(modes_hbm.at[l], modes.at[l], hbm_sem.at[0, l]),
            pltpu.make_async_copy(coupling_hbm.at[l], coupling.at[l], hbm_sem.at[1, l]),
        )
        for copy in pair:
            copy.start()
        loads.append(pair)

    barrier = pltpu.get_barrier_semaphore()
    pl.semaphore_signal(barrier, inc=1, device_id={"mode": other}, device_id_type=MESH)
    for d in range(1, ns):
        pl.semaphore_signal(
            barrier, inc=1, device_id={"sep": lax.rem(sep + d, ns)}, device_id_type=MESH
        )
    for d in range(1, nl):
        pl.semaphore_signal(
            barrier, inc=1, device_id={"leaf": lax.rem(leaf + d, nl)}, device_id_type=MESH
        )
    pl.semaphore_wait(barrier, 1 + (ns - 1) + (nl - 1))

    block[leaf, core] = start_block[0]
    block_copies = []
    for d in range(1, nl):
        copy = remote(
            start_block.at[0], block.at[leaf, core], block_ssem.at[d], block_rsem.at[d],
            leaf=lax.rem(leaf + d, nl),
        )
        copy.start()
        block_copies.append(copy)

    part_copies = []
    for l in range(leaves):
        for copy in loads[l]:
            copy.wait()
        product = contract(coupling[l], modes[l], 0, 0)
        for k in range(2):
            piece = product[:, k * half:(k + 1) * half]
            part_own[k, l] = piece
            part_send[k, l] = piece.astype(BF16)
        copy = remote(
            part_send.at[other, l], part_recv.at[l], part_ssem.at[l], part_rsem.at[l], mode=other
        )
        copy.start()
        part_copies.append(copy)

    target = [separator_of[l, 0] for l in range(leaves)]
    position = []
    for l in range(leaves):
        count = jnp.int32(0)
        for e in range(l):
            count = count + jnp.where(target[e] == target[l], 1, 0)
        position.append(count)

    for l in range(leaves):
        part_copies[l].wait()
        summed = part_own[core, l] + part_recv[l].astype(F32)
        scaled[l] = (summed / jnp.sqrt(eigenvalues[l:l + 1, :])).astype(BF16)

    slot_copies = []
    for d in range(ns):
        owner = lax.rem(sep + d, ns)
        for p in range(CAP):
            index = jnp.int32(0)
            offset = jnp.int32(-4 * rows)
            for l in range(leaves):
                mine = (target[l] == owner) & (position[l] == p)
                index = jnp.where(mine, l, index)
                offset = jnp.where(mine, row_offset[l], offset)
            slot_send[d, p] = scaled[index]
            offset_send[d, p * 8:(p + 1) * 8, :] = jnp.full((8, iface), offset, jnp.int32)
        if d > 0:
            pair = (
                remote(offset_send.at[d], offset_recv.at[d], offset_ssem.at[d], offset_rsem.at[d], sep=owner),
                remote(slot_send.at[d], slot_recv.at[d], slot_ssem.at[d], slot_rsem.at[d], sep=owner),
            )
            for copy in pair:
                copy.start()
            slot_copies.append(pair)

    for copy in block_copies:
        copy.wait()
    block_core = remote(
        block.at[:, core], block.at[:, core], core_ssem.at[0], core_rsem.at[0], mode=other
    )
    block_core.start()

    shift = lax.broadcasted_iota(jnp.int32, (rows, iface), 0) - lax.broadcasted_iota(
        jnp.int32, (rows, iface), 1
    )
    for d in range(ns):
        if d > 0:
            for copy in slot_copies[d - 1]:
                copy.wait()
        blocks, offsets = (slot_send, offset_send) if d == 0 else (slot_recv, offset_recv)
        for p in range(CAP):
            place = jnp.where(shift == offsets[d, p * 8:p * 8 + 1, :], 1.0, 0.0).astype(BF16)
            q = d * CAP + p
            padded[:, q * half:(q + 1) * half] = jnp.dot(
                place, blocks[d, p], preferred_element_type=F32
            ).astype(BF16)
    product = contract(padded[...], padded[...], 1, 1).reshape(gram.shape)
    gram[...] = product
    gram_send[...] = product.astype(BF16)

    core_copy = remote(gram_send.at[:, other], gram_recv, core_ssem.at[1], core_rsem.at[1], mode=other)
    core_copy.start()
    core_copy.wait()
    both = gram[:, core] + gram_recv[...].astype(F32)
    leaf_own[...] = both
    leaf_send[...] = both.astype(BF16)
    leaf_copies = []
    for d in range(1, nl):
        peer = lax.rem(leaf + d, nl)
        copy = remote(leaf_send.at[peer], leaf_recv.at[d], leaf_ssem.at[d], leaf_rsem.at[d], leaf=peer)
        copy.start()
        leaf_copies.append(copy)
    total = stiffness[0].astype(F32).T - leaf_own[leaf]
    for d in range(1, nl):
        leaf_copies[d - 1].wait()
        total = total - leaf_recv[d].astype(F32)
    operator[leaf, core] = total.astype(BF16)

    oper_copies = []
    for d in range(1, nl):
        copy = remote(
            operator.at[leaf, core], operator.at[leaf, core], oper_ssem.at[d], oper_rsem.at[d],
            leaf=lax.rem(leaf + d, nl),
        )
        copy.start()
        oper_copies.append(copy)
    for copy in oper_copies:
        copy.wait()
    core_copy = remote(
        operator.at[:, core], operator.at[:, core], core_ssem.at[2], core_rsem.at[2], mode=other
    )
    core_copy.start()
    block_core.wait()
    core_copy.wait()

    turned = operator[...].reshape(rows, rows)
    current = block[...].reshape(rows, cols)
    steps = rotations.shape[1]
    for k in range(steps):
        result = contract(turned, current, 0, 0)
        column_scale = jnp.sqrt(jnp.sum(result * result, 0, keepdims=True) / rows + EPSILON)
        norms[0, k:k + 1, :] = column_scale
        normed = (result / column_scale).astype(BF16)
        if k < steps - 1:
            current = jnp.dot(normed, rotations[0, k], preferred_element_type=F32).astype(BF16)
        else:
            normed_rows[...] = normed.reshape(normed_rows.shape)
            out[0] = jnp.dot(
                normed_rows[leaf, core], rotations[0, k], preferred_element_type=F32
            ).astype(BF16)


def per_device(nl, ns, nm, modes, coupling, eigenvalues, separator_of, row_offset, stiffness, start_block, rotations):
    leaves, depth, width = modes.shape
    iface = coupling.shape[2]
    half = eigenvalues.shape[1]
    rows = stiffness.shape[1]
    own, cols = start_block.shape[1:]
    steps = rotations.shape[1]
    vmem = pl.BlockSpec(memory_space=pltpu.VMEM)
    smem = pl.BlockSpec(memory_space=pltpu.SMEM)
    hbm = pl.BlockSpec(memory_space=pl.ANY)
    dma = pltpu.SemaphoreType.DMA
    scratch = [
        pltpu.VMEM((leaves, depth, width), BF16),
        pltpu.VMEM((leaves, depth, iface), BF16),
        pltpu.VMEM((nm, leaves, iface, half), F32),
        pltpu.VMEM((nm, leaves, iface, half), BF16),
        pltpu.VMEM((leaves, iface, half), BF16),
        pltpu.VMEM((leaves, iface, half), BF16),
        pltpu.VMEM((ns, CAP, iface, half), BF16),
        pltpu.VMEM((ns, CAP, iface, half), BF16),
        pltpu.VMEM((ns, CAP * 8, iface), jnp.int32),
        pltpu.VMEM((ns, CAP * 8, iface), jnp.int32),
        pltpu.VMEM((rows, ns * CAP * half), BF16),
        pltpu.VMEM((nl, nm, own, rows), F32),
        pltpu.VMEM((nl, nm, own, rows), BF16),
        pltpu.VMEM((nl, own, rows), BF16),
        pltpu.VMEM((nl, own, rows), F32),
        pltpu.VMEM((nl, own, rows), BF16),
        pltpu.VMEM((nl, own, rows), BF16),
        pltpu.VMEM((nl, nm, own, rows), BF16),
        pltpu.VMEM((nl, nm, own, cols), BF16),
        pltpu.VMEM((nl, nm, own, cols), BF16),
        dma((2, leaves)),
        dma((leaves,)), dma((leaves,)),
        dma((nl,)), dma((nl,)),
        dma((ns,)), dma((ns,)),
        dma((ns,)), dma((ns,)),
        dma((nl,)), dma((nl,)),
        dma((nl,)), dma((nl,)),
        dma((3,)), dma((3,)),
    ]
    return pl.pallas_call(
        functools.partial(kernel, nl, ns),
        out_shape=(
            jax.ShapeDtypeStruct((1, own, cols), BF16),
            jax.ShapeDtypeStruct((1, steps, cols), F32),
        ),
        in_specs=[smem, smem, hbm, hbm, vmem, vmem, vmem, vmem],
        out_specs=(vmem, vmem),
        scratch_shapes=scratch,
        compiler_params=pltpu.CompilerParams(
            collective_id=0, has_side_effects=True, vmem_limit_bytes=48 * 1024 * 1024
        ),
    )(separator_of, row_offset, modes, coupling, eigenvalues, stiffness, start_block, rotations)


def solution(mesh):
    in_specs = (
        P(("leaf", "sep"), "mode", None),
        P(("leaf", "sep"), "mode", None),
        P(("leaf", "sep"), "mode"),
        P(("leaf", "sep"), None),
        P(("leaf", "sep")),
        P("sep", None, ("leaf", "mode")),
        P("sep", ("leaf", "mode"), None),
        P("sep", None, None, None),
    )
    out_specs = (P("sep", ("leaf", "mode"), None), P("sep", None, None))
    shape = mesh.shape
    return jax.shard_map(
        functools.partial(per_device, shape["leaf"], shape["sep"], shape["mode"]),
        mesh=mesh, in_specs=in_specs, out_specs=out_specs, check_vma=False,
    )
```

time: 243 us -> 48.1 us (0.20)
  waiting for transfers between devices: 77.6 us -> 0 us
  blocking collectives: 42.9 us -> 0 us
  Pallas kernels: 0 us -> 38.4 us
  local copies, waits for them, and re-layouts: 44.6 us -> 8.11 us
  loops' own time: 31.8 us -> 0 us
  matrix products: 15.6 us -> 0 us
  between operations: 13.9 us -> 0.66 us
  starting transfers between devices: 11.3 us -> 0 us
  other arithmetic: 3.86 us -> 0 us
    reduce_scatter x2 -> x0, waiting for transfers between devices: 38.5 us -> none  [the longest x1 33.3 us: per_device(): lax.psum_scatter(assemble_rows(jnp.int32(0), lax.axis_size(('leaf', 'mode...]
    pallas_call x0 -> x1, Pallas kernels: none -> 38.4 us  [per_device(): pl.pallas_call(functools.partial(kernel, nl, ns), out_shape=(jax.ShapeDty...]
    unnamed x4 -> x0, waiting for transfers between devices: 34.8 us -> none
    another operation x2 -> x0, loops' own time: 31.8 us -> none  [coupled_correction(): return lax.fori_loop(0, blocks.shape[0], add_slot, initial)]
    dynamic_update_slice x24 -> x0, local copies, waits for them, and re-layouts: 27.9 us -> none  [add_slot(): lax.dynamic_update_slice_in_dim(accumulated, current + update, offset, 0)]
    psum x2 -> x0, blocking collectives: 24.4 us -> none  [per_device(): squares = lax.psum(jnp.sum(summed * summed, 0), ('leaf', 'mode'))]
    all_gather x2 -> x0, blocking collectives: 18.5 us -> none  [gather_rows(): return lax.all_gather(own_block, ('leaf', 'mode'), axis=0, tiled=True)]
    dot_general x22 -> x0, matrix products: 15.6 us -> none  [the longest x1 6.22 us: leaf_projection(): jnp.einsum('ldm,ldw->mlw', modes, coupling, preferred_element_type=jnp.fl...]
  transfers between devices with their start and end apart: 5 -> 0, of which waited for: 4 -> 0; matrix products, arithmetic and copies ran while one was open for 2% -> 0% of each run, Pallas kernels for 0% -> 0%
where the time goes in v1:
time: 48.1 us; the launch traced here: 47.1 us
  Pallas kernels  38.4 us (80%)
  local copies, waits for them, and re-layouts  8.11 us (17%)
  between operations  0.66 us (1%)
    pallas_call x1, Pallas kernels, per_device(): pl.pallas_call(functools.partial(kernel, nl, ns), out_shape=(jax.ShapeDty...  38.4 us
    unnamed x14, local copies, waits for them, and re-layouts  8.11 us

profile of v1, /device:TPU:0, one launch (start us, length us, event | category | flops | bytes accessed | tf_op | source)
XLA Modules:
  0.0 47.1 jit_solution(12354832056874220341)
XLA Ops:
  0.6 0.7 %copy.10.separator_of = s32[8,1]{1,0:T(8,128)S(1)} copy(s32[8,1]{0,1:T(1,128)} %param.11) | data formatting | bytes 64 | tf_op args[3]
  1.4 1.0 %copy.11.stiffness = bf16[1,512,64]{2,1,0:T(8,128)(2,1)S(1)} copy(bf16[1,512,64]{1,2,0:T(8,128)(2,1)} %param.13) | data formatting | bytes 131072 | tf_op args[5]
  2.3 0.0 copy-start
  2.3 2.2 %copy-done = bf16[8,1024,256]{2,1,0:T(8,128)(2,1)S(1)} copy-done((bf16[8,1024,256]{2,1,0:T(8,128)(2,1)S(1)}, bf16[8,1024,256]{2,1,0:T(8,128)(2,1)}, u32[]{:S(2)}) %copy-start) | copy-done | bytes 4194328
  4.5 0.0 copy-start.1
  4.5 0.9 %copy-done.1 = bf16[1,2,256,256]{3,2,1,0:T(8,128)(2,1)S(1)} copy-done((bf16[1,2,256,256]{3,2,1,0:T(8,128)(2,1)S(1)}, bf16[1,2,256,256]{3,2,1,0:T(8,128)(2,1)}, u32[]{:S(2)}) %copy-start.1) | copy-done | bytes 262168
  5.5 0.0 copy-start.2
  5.5 0.8 %copy-done.2 = bf16[1,64,256]{2,1,0:T(8,128)(2,1)S(1)} copy-done((bf16[1,64,256]{2,1,0:T(8,128)(2,1)S(1)}, bf16[1,64,256]{2,1,0:T(8,128)(2,1)}, u32[]{:S(2)}) %copy-start.2) | copy-done | bytes 32792
  6.2 0.0 copy-start.3
  6.2 0.7 %copy-done.3 = f32[8,128]{1,0:T(8,128)S(1)} copy-done((f32[8,128]{1,0:T(8,128)S(1)}, f32[8,128]{1,0:T(8,128)}, u32[]{:S(2)}) %copy-start.3) | copy-done | bytes 4120
  6.9 0.0 copy-start.4
  6.9 0.7 %copy-done.4 = s32[8]{0:T(128)S(1)} copy-done((s32[8]{0:T(128)S(1)}, s32[8]{0:T(128)}, u32[]{:S(2)}) %copy-start.4) | copy-done | bytes 56
  7.6 38.4 %shard_map.95 = (bf16[1,64,256]{2,1,0:T(8,128)(2,1)S(1)}, f32[1,2,256]{2,1,0:T(2,128)S(1)}) custom-call(s32[8,1]{1,0:T(8,128)S(1)} %copy.10.separator_of, s32[8]{0:T(128)S(1)} %copy-done.4, bf16[8,1024,256]{2,1,0:T(8,128)(2,1)S(1)} %copy-done, bf16[8,1024,256]{2,1,0:T(8,128)(2,1)} %coupling_hbm.1, f32[8,128]{1,0:T(8,128)S(1)} %copy-done.3, ...), custom_call_target="tpu_custom_call" | custom-call | tf_op jit(solution)/shard_map/pallas_call | solution.py:248
  46.0 0.6 %copy.14 = bf16[1,64,256]{2,1,0:T(8,128)(2,1)} copy(bf16[1,64,256]{2,1,0:T(8,128)(2,1)S(1)} %get-tuple-element.4) | data formatting | bytes 65536
  46.6 0.6 %copy.15 = f32[1,2,256]{2,1,0:T(2,128)} copy(f32[1,2,256]{2,1,0:T(2,128)S(1)} %get-tuple-element.5) | data formatting | bytes 4096
Async XLA Ops:
  2.3 2.2 %copy-start = (bf16[8,1024,256]{2,1,0:T(8,128)(2,1)S(1)}, bf16[8,1024,256]{2,1,0:T(8,128)(2,1)}, u32[]{:S(2)}) copy-start(bf16[8,1024,256]{2,1,0:T(8,128)(2,1)} %modes_hbm.1) | copy-start | bytes 12582916
  4.5 0.9 %copy-start.1 = (bf16[1,2,256,256]{3,2,1,0:T(8,128)(2,1)S(1)}, bf16[1,2,256,256]{3,2,1,0:T(8,128)(2,1)}, u32[]{:S(2)}) copy-start(bf16[1,2,256,256]{3,2,1,0:T(8,128)(2,1)} %rotations.1) | copy-start | bytes 786436
  5.5 0.8 %copy-start.2 = (bf16[1,64,256]{2,1,0:T(8,128)(2,1)S(1)}, bf16[1,64,256]{2,1,0:T(8,128)(2,1)}, u32[]{:S(2)}) copy-start(bf16[1,64,256]{2,1,0:T(8,128)(2,1)} %start_block.1) | copy-start | bytes 98308
  6.2 0.7 %copy-start.3 = (f32[8,128]{1,0:T(8,128)S(1)}, f32[8,128]{1,0:T(8,128)}, u32[]{:S(2)}) copy-start(f32[8,128]{1,0:T(8,128)} %eigenvalues.1) | copy-start | bytes 12292
  6.9 0.7 %copy-start.4 = (s32[8]{0:T(128)S(1)}, s32[8]{0:T(128)}, u32[]{:S(2)}) copy-start(s32[8]{0:T(128)} %row_offset.1) | copy-start | bytes 100

commit v2 on v1

v2 whole, which is shorter than its diff:
```python
import functools

import jax
import jax.numpy as jnp
from jax import lax
from jax.experimental import pallas as pl
from jax.experimental.pallas import tpu as pltpu
from jax.sharding import PartitionSpec as P

CAP = 2
EPSILON = 1e-06
MESH = pl.DeviceIdType.MESH
F32 = jnp.float32
BF16 = jnp.bfloat16


def remote(src, dst, send_sem, recv_sem, **device):
    return pltpu.make_async_remote_copy(
        src_ref=src,
        dst_ref=dst,
        send_sem=send_sem,
        recv_sem=recv_sem,
        device_id=device,
        device_id_type=MESH,
    )


def contract(a, b, dim_a, dim_b):
    return lax.dot_general(a, b, (((dim_a,), (dim_b,)), ((), ())), preferred_element_type=F32)


def partner(me, distance, count):
    if count & (count - 1):
        return lax.rem(me + distance, count)
    total = jnp.int32(0)
    bit = 1
    while bit < count:
        total = total + (me // bit + distance // bit) % 2 * bit
        bit *= 2
    return total


def kernel(
    nl, ns,
    separator_of, row_offset, modes_hbm, coupling_hbm, eigenvalues_hbm, stiffness_hbm, start_hbm, rotations_hbm,
    out, norms,
    targets, starts, eigenvalues, stiffness, start_block, rotations,
    modes, coupling, part_own, part_send, part_recv,
    slot_send, slot_recv, offset_send, offset_recv, padded,
    gram, gram_send, gram_recv, leaf_send, leaf_recv, operator, block, normed_rows,
    small_sem, hbm_sem, part_ssem, part_rsem, block_ssem, block_rsem, slot_ssem, slot_rsem,
    offset_ssem, offset_rsem, gram_ssem, gram_rsem, leaf_ssem, leaf_rsem, oper_ssem, oper_rsem,
    core_ssem, core_rsem,
):
    leaf, sep, core = lax.axis_index("leaf"), lax.axis_index("sep"), lax.axis_index("mode")
    other = 1 - core
    leaves = modes.shape[0]
    iface, half = slot_send.shape[2:]
    rows = padded.shape[0]
    own, cols = start_block.shape[1:]

    smalls = []
    for k, (src, dst) in enumerate((
        (separator_of, targets), (row_offset, starts), (start_hbm, start_block),
        (eigenvalues_hbm, eigenvalues), (stiffness_hbm, stiffness), (rotations_hbm, rotations),
    )):
        copy = pltpu.make_async_copy(src, dst, small_sem.at[k])
        copy.start()
        smalls.append(copy)
    loads = []
    for l in range(leaves):
        for k, (src, dst) in enumerate(((modes_hbm, modes), (coupling_hbm, coupling))):
            copy = pltpu.make_async_copy(src.at[l], dst.at[l], hbm_sem.at[k, l])
            copy.start()
            loads.append(copy)

    barrier = pltpu.get_barrier_semaphore()
    pl.semaphore_signal(barrier, inc=1, device_id={"mode": other}, device_id_type=MESH)
    for d in range(1, ns):
        pl.semaphore_signal(
            barrier, inc=1, device_id={"sep": partner(sep, d, ns)}, device_id_type=MESH
        )
    for d in range(1, nl):
        pl.semaphore_signal(
            barrier, inc=1, device_id={"leaf": lax.rem(leaf + d, nl)}, device_id_type=MESH
        )
    smalls[0].wait()
    smalls[1].wait()

    target = [targets[l] for l in range(leaves)]
    position = []
    for l in range(leaves):
        count = jnp.int32(0)
        for e in range(l):
            count = count + jnp.where(target[e] == target[l], 1, 0)
        position.append(count)
    order = list(range(ns // 2, ns)) + list(range(1, ns // 2)) + [0]
    slots = []
    for d in order:
        owner = partner(sep, d, ns)
        for p in range(CAP):
            index = jnp.int32(0)
            offset = jnp.int32(-4 * rows)
            for l in range(leaves):
                mine = (target[l] == owner) & (position[l] == p)
                index = jnp.where(mine, l, index)
                offset = jnp.where(mine, starts[l], offset)
            offset_send[d, p:p + 1, :] = jnp.full((1, iface), offset, jnp.int32)
            slots.append((d, p, owner, index))
    pl.semaphore_wait(barrier, 1 + (ns - 1) + (nl - 1))
    offset_copies = {}
    for d in order[:-1]:
        copy = remote(
            offset_send.at[d], offset_recv.at[d], offset_ssem.at[d], offset_rsem.at[d],
            sep=partner(sep, d, ns),
        )
        copy.start()
        offset_copies[d] = copy

    smalls[2].wait()
    block[leaf, core] = start_block[0]
    block_copies = []
    for d in range(1, nl):
        copy = remote(
            start_block.at[0], block.at[leaf, core], block_ssem.at[d], block_rsem.at[d],
            leaf=lax.rem(leaf + d, nl),
        )
        copy.start()
        block_copies.append(copy)

    smalls[3].wait()
    for copy in loads:
        copy.wait()
    part_copies = []
    slot_copies = {}

    def finish(q):
        d, p, owner, index = slots[q]
        part_copies[q].wait()
        summed = part_own[core, q] + part_recv[q].astype(F32)
        slot_send[d, p] = (summed / jnp.sqrt(eigenvalues[pl.ds(index, 1), :])).astype(BF16)
        if d > 0:
            copy = remote(
                slot_send.at[d, p], slot_recv.at[d, p], slot_ssem.at[d, p], slot_rsem.at[d, p], sep=owner
            )
            copy.start()
            slot_copies[d, p] = copy

    for q, (d, p, owner, index) in enumerate(slots):
        product = contract(coupling[index], modes[index], 0, 0)
        for k in range(2):
            piece = product[:, k * half:(k + 1) * half]
            part_own[k, q] = piece
            part_send[k, q] = piece.astype(BF16)
        copy = remote(
            part_send.at[other, q], part_recv.at[q], part_ssem.at[q], part_rsem.at[q], mode=other
        )
        copy.start()
        part_copies.append(copy)
        if q > 0:
            finish(q - 1)
    finish(len(slots) - 1)

    for copy in block_copies:
        copy.wait()
    block_core = remote(
        block.at[:, core], block.at[:, core], core_ssem.at[nl], core_rsem.at[nl], mode=other
    )
    block_core.start()

    shift = lax.broadcasted_iota(jnp.int32, (rows, iface), 0) - lax.broadcasted_iota(
        jnp.int32, (rows, iface), 1
    )
    for d in [0] + order[:-1]:
        blocks, offsets = (slot_send, offset_send) if d == 0 else (slot_recv, offset_recv)
        if d > 0:
            offset_copies[d].wait()
        for p in range(CAP):
            if d > 0:
                slot_copies[d, p].wait()
            place = jnp.where(shift == offsets[d, p:p + 1, :], 1.0, 0.0).astype(BF16)
            q = d * CAP + p
            padded[:, q * half:(q + 1) * half] = jnp.dot(
                place, blocks[d, p], preferred_element_type=F32
            ).astype(BF16)

    gram_copies = []
    peers = [lax.rem(leaf + d, nl) for d in list(range(1, nl)) + [0]]
    pair_rows = 2 * own
    for d, peer in enumerate(peers):
        chunk = padded[pl.ds(pl.multiple_of(peer * pair_rows, pair_rows), pair_rows), :]
        product = contract(chunk, padded[...], 1, 1).reshape(2, own, rows)
        gram[d] = product
        gram_send[d] = product.astype(BF16)
        copy = remote(
            gram_send.at[d, other], gram_recv.at[d], gram_ssem.at[d], gram_rsem.at[d], mode=other
        )
        copy.start()
        gram_copies.append(copy)
    leaf_copies = []
    for d, peer in enumerate(peers[:-1]):
        gram_copies[d].wait()
        leaf_send[d] = (gram[d, core] + gram_recv[d].astype(F32)).astype(BF16)
        copy = remote(leaf_send.at[d], leaf_recv.at[d], leaf_ssem.at[d], leaf_rsem.at[d], leaf=peer)
        copy.start()
        leaf_copies.append(copy)
    smalls[4].wait()
    gram_copies[nl - 1].wait()
    total = stiffness[0].astype(F32) - (gram[nl - 1, core] + gram_recv[nl - 1].astype(F32))
    for d in range(nl - 1):
        leaf_copies[d].wait()
        total = total - leaf_recv[d].astype(F32)
    operator[leaf, core] = total.astype(BF16)

    oper_copies = []
    for d in range(1, nl):
        copy = remote(
            operator.at[leaf, core], operator.at[leaf, core], oper_ssem.at[d], oper_rsem.at[d],
            leaf=lax.rem(leaf + d, nl),
        )
        copy.start()
        oper_copies.append(copy)
    core_copies = []
    for d in range(nl):
        if d > 0:
            oper_copies[d - 1].wait()
        source = lax.rem(leaf - d + nl, nl)
        copy = remote(
            operator.at[source, core], operator.at[source, core], core_ssem.at[d], core_rsem.at[d], mode=other
        )
        copy.start()
        core_copies.append(copy)
    block_core.wait()
    smalls[5].wait()
    for copy in core_copies:
        copy.wait()

    turned = operator[...].reshape(rows, rows).T
    current = block[...].reshape(rows, cols)
    steps = rotations.shape[1]
    for k in range(steps):
        result = jnp.dot(turned, current, preferred_element_type=F32)
        column_scale = jnp.sqrt(jnp.sum(result * result, 0, keepdims=True) / rows + EPSILON)
        norms[0, k:k + 1, :] = column_scale
        normed = (result / column_scale).astype(BF16)
        if k < steps - 1:
            current = jnp.dot(normed, rotations[0, k], preferred_element_type=F32).astype(BF16)
        else:
            normed_rows[...] = normed.reshape(normed_rows.shape)
            out[0] = jnp.dot(
                normed_rows[leaf, core], rotations[0, k], preferred_element_type=F32
            ).astype(BF16)


def per_device(nl, ns, nm, modes, coupling, eigenvalues, separator_of, row_offset, stiffness, start_block, rotations):
    leaves, depth, width = modes.shape
    iface = coupling.shape[2]
    half = eigenvalues.shape[1]
    rows = stiffness.shape[1]
    own, cols = start_block.shape[1:]
    steps = rotations.shape[1]
    vmem = pl.BlockSpec(memory_space=pltpu.VMEM)
    hbm = pl.BlockSpec(memory_space=pl.ANY)
    dma = pltpu.SemaphoreType.DMA
    slots = ns * CAP
    scratch = [
        pltpu.SMEM((leaves,), jnp.int32),
        pltpu.SMEM((leaves,), jnp.int32),
        pltpu.VMEM((leaves, half), F32),
        pltpu.VMEM((1, own, rows), BF16),
        pltpu.VMEM((1, own, cols), BF16),
        pltpu.VMEM((1, steps, cols, cols), BF16),
        pltpu.VMEM((leaves, depth, width), BF16),
        pltpu.VMEM((leaves, depth, iface), BF16),
        pltpu.VMEM((nm, slots, iface, half), F32),
        pltpu.VMEM((nm, slots, iface, half), BF16),
        pltpu.VMEM((slots, iface, half), BF16),
        pltpu.VMEM((ns, CAP, iface, half), BF16),
        pltpu.VMEM((ns, CAP, iface, half), BF16),
        pltpu.VMEM((ns, 8, iface), jnp.int32),
        pltpu.VMEM((ns, 8, iface), jnp.int32),
        pltpu.VMEM((rows, slots * half), BF16),
        pltpu.VMEM((nl, nm, own, rows), F32),
        pltpu.VMEM((nl, nm, own, rows), BF16),
        pltpu.VMEM((nl, own, rows), BF16),
        pltpu.VMEM((nl, own, rows), BF16),
        pltpu.VMEM((nl, own, rows), BF16),
        pltpu.VMEM((nl, nm, own, rows), BF16),
        pltpu.VMEM((nl, nm, own, cols), BF16),
        pltpu.VMEM((nl, nm, own, cols), BF16),
        dma((6,)),
        dma((2, leaves)),
        dma((slots,)), dma((slots,)),
        dma((nl,)), dma((nl,)),
        dma((ns, CAP)), dma((ns, CAP)),
        dma((ns,)), dma((ns,)),
        dma((nl,)), dma((nl,)),
        dma((nl,)), dma((nl,)),
        dma((nl,)), dma((nl,)),
        dma((nl + 1,)), dma((nl + 1,)),
    ]
    return pl.pallas_call(
        functools.partial(kernel, nl, ns),
        out_shape=(
            jax.ShapeDtypeStruct((1, own, cols), BF16),
            jax.ShapeDtypeStruct((1, steps, cols), F32),
        ),
        in_specs=[hbm] * 8,
        out_specs=(vmem, vmem),
        scratch_shapes=scratch,
        compiler_params=pltpu.CompilerParams(
            collective_id=0, has_side_effects=True, vmem_limit_bytes=60 * 1024 * 1024
        ),
    )(
        separator_of.reshape(leaves), row_offset, modes, coupling, eigenvalues,
        jnp.swapaxes(stiffness, 1, 2), start_block, rotations,
    )


def solution(mesh):
    in_specs = (
        P(("leaf", "sep"), "mode", None),
        P(("leaf", "sep"), "mode", None),
        P(("leaf", "sep"), "mode"),
        P(("leaf", "sep"), None),
        P(("leaf", "sep")),
        P("sep", None, ("leaf", "mode")),
        P("sep", ("leaf", "mode"), None),
        P("sep", None, None, None),
    )
    out_specs = (P("sep", ("leaf", "mode"), None), P("sep", None, None))
    shape = mesh.shape
    return jax.shard_map(
        functools.partial(per_device, shape["leaf"], shape["sep"], shape["mode"]),
        mesh=mesh, in_specs=in_specs, out_specs=out_specs, check_vma=False,
    )
```

time: 48.1 us -> 39.3 us (0.82); the launches traced: 47.1 us -> 39.1 us
  local copies, waits for them, and re-layouts: 8.11 us -> 2.62 us
  Pallas kernels: 38.4 us -> 35.9 us
    unnamed x14 -> x2, local copies, waits for them, and re-layouts: 8.11 us -> 2.62 us
    pallas_call x1, Pallas kernels: 38.4 us -> 35.9 us  [per_device(): pl.pallas_call(functools.partial(kernel, nl, ns), out_shape=(jax.ShapeDty...]
where the time goes in v2:
time: 39.3 us; the launch traced here: 39.1 us
  Pallas kernels  35.9 us (91%)
  local copies, waits for them, and re-layouts  2.62 us (7%)
  between operations  0.64 us (2%)
    pallas_call x1, Pallas kernels, per_device(): pl.pallas_call(functools.partial(kernel, nl, ns), out_shape=(jax.ShapeDty...  35.9 us
    unnamed x2, local copies, waits for them, and re-layouts  2.62 us

profile of v2, /device:TPU:0, one launch (start us, length us, event | category | flops | bytes accessed | tf_op | source)
XLA Modules:
  0.0 39.1 jit_solution(15083959780065335520)
XLA Ops:
  0.6 35.9 %shard_map.95 = (bf16[1,64,256]{2,1,0:T(8,128)(2,1)}, f32[1,2,256]{2,1,0:T(2,128)}) custom-call(s32[8]{0:T(128)} %bitcast.3, s32[8]{0:T(128)} %row_offset.1, bf16[8,1024,256]{2,1,0:T(8,128)(2,1)} %modes_hbm.1, bf16[8,1024,256]{2,1,0:T(8,128)(2,1)} %coupling_hbm.1, f32[8,128]{1,0:T(8,128)} %eigenvalues_hbm.1, bf16[1,64,512]{2,1,0:T(8,128)(2,1)} %bitcast.2, ...), custom_call_target="tpu_custom_call" | custom-call | tf_op jit(solution)/shard_map/pallas_call | solution.py:302
  36.5 1.4 %copy.12 = bf16[1,64,256]{2,1,0:T(8,128)(2,1)} copy(bf16[1,64,256]{2,1,0:T(8,128)(2,1)} %get-tuple-element.4) | data formatting | bytes 65536
  37.9 1.2 %copy.13 = f32[1,2,256]{2,1,0:T(2,128)} copy(f32[1,2,256]{2,1,0:T(2,128)} %get-tuple-element.5) | data formatting | bytes 4096

commit v3 on v2

--- a/solution.py
+++ b/solution.py
@@ -45,18 +45,20 @@
     separator_of, row_offset, modes_hbm, coupling_hbm, eigenvalues_hbm, stiffness_hbm, start_hbm, rotations_hbm,
     out, norms,
     targets, starts, eigenvalues, stiffness, start_block, rotations,
-    modes, coupling, part_own, part_send, part_recv,
-    slot_send, slot_recv, offset_send, offset_recv, padded,
+    modes, coupling, eigen_both, part_send, part_recv, scales,
+    slot_send, slot_recv, offset_send, offset_recv, placed, places,
     gram, gram_send, gram_recv, leaf_send, leaf_recv, operator, block, normed_rows,
     small_sem, hbm_sem, part_ssem, part_rsem, block_ssem, block_rsem, slot_ssem, slot_rsem,
     offset_ssem, offset_rsem, gram_ssem, gram_rsem, leaf_ssem, leaf_rsem, oper_ssem, oper_rsem,
-    core_ssem, core_rsem,
+    core_ssem, core_rsem, eigen_ssem, eigen_rsem,
 ):
     leaf, sep, core = lax.axis_index("leaf"), lax.axis_index("sep"), lax.axis_index("mode")
     other = 1 - core
     leaves = modes.shape[0]
-    iface, half = slot_send.shape[2:]
-    rows = padded.shape[0]
+    iface = coupling.shape[2]
+    tile = iface // 2
+    half = eigenvalues.shape[1]
+    rows = placed.shape[0]
     own, cols = start_block.shape[1:]
 
     smalls = []
@@ -98,15 +100,17 @@
     slots = []
     for d in order:
         owner = partner(sep, d, ns)
-        for p in range(CAP):
+        found = []
+        for p in (other, core):
             index = jnp.int32(0)
             offset = jnp.int32(-4 * rows)
             for l in range(leaves):
                 mine = (target[l] == owner) & (position[l] == p)
                 index = jnp.where(mine, l, index)
                 offset = jnp.where(mine, starts[l], offset)
-            offset_send[d, p:p + 1, :] = jnp.full((1, iface), offset, jnp.int32)
-            slots.append((d, p, owner, index))
+            found.append(index)
+        offset_send[d] = jnp.full(offset_send.shape[1:], offset, jnp.int32)
+        slots.append((d, owner, found[0], found[1]))
     pl.semaphore_wait(barrier, 1 + (ns - 1) + (nl - 1))
     offset_copies = {}
     for d in order[:-1]:
@@ -129,37 +133,31 @@
         block_copies.append(copy)
 
     smalls[3].wait()
+    eigen_both[core] = eigenvalues[...]
+    eigen_copy = remote(eigenvalues, eigen_both.at[core], eigen_ssem, eigen_rsem, mode=other)
+    eigen_copy.start()
+
     for copy in loads:
         copy.wait()
-    part_copies = []
+    eigen_copy.wait()
+    for k in range(2):
+        scales[:, k * half:(k + 1) * half] = 1.0 / jnp.sqrt(eigen_both[k])
     slot_copies = {}
-
-    def finish(q):
-        d, p, owner, index = slots[q]
-        part_copies[q].wait()
-        summed = part_own[core, q] + part_recv[q].astype(F32)
-        slot_send[d, p] = (summed / jnp.sqrt(eigenvalues[pl.ds(index, 1), :])).astype(BF16)
+    for d, owner, given, kept in slots:
+        part_send[d] = contract(coupling[given], modes[given], 0, 0).astype(BF16)
+        part_copy = remote(part_send.at[d], part_recv.at[d], part_ssem.at[d], part_rsem.at[d], mode=other)
+        part_copy.start()
+        product = contract(coupling[kept], modes[kept], 0, 0)
+        part_copy.wait()
+        scaled = ((product + part_recv[d].astype(F32)) * scales[pl.ds(kept, 1), :]).astype(BF16)
+        square = contract(scaled, scaled, 1, 1).astype(BF16)
+        slot_send[d, 0] = square[:tile, :tile]
+        slot_send[d, 1] = square[tile:, :tile]
+        slot_send[d, 2] = square[tile:, tile:]
         if d > 0:
-            copy = remote(
-                slot_send.at[d, p], slot_recv.at[d, p], slot_ssem.at[d, p], slot_rsem.at[d, p], sep=owner
-            )
+            copy = remote(slot_send.at[d], slot_recv.at[d], slot_ssem.at[d], slot_rsem.at[d], sep=owner)
             copy.start()
-            slot_copies[d, p] = copy
-
-    for q, (d, p, owner, index) in enumerate(slots):
-        product = contract(coupling[index], modes[index], 0, 0)
-        for k in range(2):
-            piece = product[:, k * half:(k + 1) * half]
-            part_own[k, q] = piece
-            part_send[k, q] = piece.astype(BF16)
-        copy = remote(
-            part_send.at[other, q], part_recv.at[q], part_ssem.at[q], part_rsem.at[q], mode=other
-        )
-        copy.start()
-        part_copies.append(copy)
-        if q > 0:
-            finish(q - 1)
-    finish(len(slots) - 1)
+            slot_copies[d] = copy
 
     for copy in block_copies:
         copy.wait()
@@ -175,21 +173,24 @@
         blocks, offsets = (slot_send, offset_send) if d == 0 else (slot_recv, offset_recv)
         if d > 0:
             offset_copies[d].wait()
-        for p in range(CAP):
-            if d > 0:
-                slot_copies[d, p].wait()
-            place = jnp.where(shift == offsets[d, p:p + 1, :], 1.0, 0.0).astype(BF16)
-            q = d * CAP + p
-            padded[:, q * half:(q + 1) * half] = jnp.dot(
-                place, blocks[d, p], preferred_element_type=F32
-            ).astype(BF16)
+        place = jnp.where(shift == offsets[d, 0:1, :], 1.0, 0.0).astype(BF16)
+        places[:, d * iface:(d + 1) * iface] = place
+        if d > 0:
+            slot_copies[d].wait()
+        corner = blocks[d, 1]
+        top = jnp.concatenate([blocks[d, 0], corner.T], axis=1)
+        low = jnp.concatenate([corner, blocks[d, 2]], axis=1)
+        placed[:, d * iface:(d + 1) * iface] = (
+            jnp.dot(place[:, :tile], top, preferred_element_type=F32)
+            + jnp.dot(place[:, tile:], low, preferred_element_type=F32)
+        ).astype(BF16)
 
     gram_copies = []
     peers = [lax.rem(leaf + d, nl) for d in list(range(1, nl)) + [0]]
     pair_rows = 2 * own
     for d, peer in enumerate(peers):
-        chunk = padded[pl.ds(pl.multiple_of(peer * pair_rows, pair_rows), pair_rows), :]
-        product = contract(chunk, padded[...], 1, 1).reshape(2, own, rows)
+        chunk = placed[pl.ds(pl.multiple_of(peer * pair_rows, pair_rows), pair_rows), :]
+        product = contract(chunk, places[...], 1, 1).reshape(2, own, rows)
         gram[d] = product
         gram_send[d] = product.astype(BF16)
         copy = remote(
@@ -242,7 +243,7 @@
         result = jnp.dot(turned, current, preferred_element_type=F32)
         column_scale = jnp.sqrt(jnp.sum(result * result, 0, keepdims=True) / rows + EPSILON)
         norms[0, k:k + 1, :] = column_scale
-        normed = (result / column_scale).astype(BF16)
+        normed = (result * (1.0 / column_scale)).astype(BF16)
         if k < steps - 1:
             current = jnp.dot(normed, rotations[0, k], preferred_element_type=F32).astype(BF16)
         else:
@@ -262,7 +263,7 @@
     vmem = pl.BlockSpec(memory_space=pltpu.VMEM)
     hbm = pl.BlockSpec(memory_space=pl.ANY)
     dma = pltpu.SemaphoreType.DMA
-    slots = ns * CAP
+    assert nm == CAP
     scratch = [
         pltpu.SMEM((leaves,), jnp.int32),
         pltpu.SMEM((leaves,), jnp.int32),
@@ -272,14 +273,16 @@
         pltpu.VMEM((1, steps, cols, cols), BF16),
         pltpu.VMEM((leaves, depth, width), BF16),
         pltpu.VMEM((leaves, depth, iface), BF16),
-        pltpu.VMEM((nm, slots, iface, half), F32),
-        pltpu.VMEM((nm, slots, iface, half), BF16),
-        pltpu.VMEM((slots, iface, half), BF16),
-        pltpu.VMEM((ns, CAP, iface, half), BF16),
-        pltpu.VMEM((ns, CAP, iface, half), BF16),
+        pltpu.VMEM((nm, leaves, half), F32),
+        pltpu.VMEM((ns, iface, width), BF16),
+        pltpu.VMEM((ns, iface, width), BF16),
+        pltpu.VMEM((leaves, width), F32),
+        pltpu.VMEM((ns, 3, iface // 2, iface // 2), BF16),
+        pltpu.VMEM((ns, 3, iface // 2, iface // 2), BF16),
         pltpu.VMEM((ns, 8, iface), jnp.int32),
         pltpu.VMEM((ns, 8, iface), jnp.int32),
-        pltpu.VMEM((rows, slots * half), BF16),
+        pltpu.VMEM((rows, ns * iface), BF16),
+        pltpu.VMEM((rows, ns * iface), BF16),
         pltpu.VMEM((nl, nm, own, rows), F32),
         pltpu.VMEM((nl, nm, own, rows), BF16),
         pltpu.VMEM((nl, own, rows), BF16),
@@ -290,14 +293,15 @@
         pltpu.VMEM((nl, nm, own, cols), BF16),
         dma((6,)),
         dma((2, leaves)),
-        dma((slots,)), dma((slots,)),
+        dma((ns,)), dma((ns,)),
         dma((nl,)), dma((nl,)),
-        dma((ns, CAP)), dma((ns, CAP)),
+        dma((ns,)), dma((ns,)),
         dma((ns,)), dma((ns,)),
         dma((nl,)), dma((nl,)),
         dma((nl,)), dma((nl,)),
         dma((nl,)), dma((nl,)),
         dma((nl + 1,)), dma((nl + 1,)),
+        dma, dma,
     ]
     return pl.pallas_call(
         functools.partial(kernel, nl, ns),

time: 39.3 us -> 38.4 us (0.977)
  Pallas kernels: 35.9 us -> 34.9 us
    pallas_call x1, Pallas kernels: 35.9 us -> 34.9 us  [per_device(): pl.pallas_call(functools.partial(kernel, nl, ns), out_shape=(jax.ShapeDty...]
where the time goes in v3:
time: 38.4 us; the launch traced here: 38.2 us
  Pallas kernels  34.9 us (91%)
  local copies, waits for them, and re-layouts  2.62 us (7%)
  between operations  0.64 us (2%)
    pallas_call x1, Pallas kernels, per_device(): pl.pallas_call(functools.partial(kernel, nl, ns), out_shape=(jax.ShapeDty...  34.9 us
    unnamed x2, local copies, waits for them, and re-layouts  2.62 us

profile of v3, /device:TPU:0, one launch (start us, length us, event | category | flops | bytes accessed | tf_op | source)
XLA Modules:
  0.0 38.2 jit_solution(3813410961383981227)
XLA Ops:
  0.6 34.9 %shard_map.95 = (bf16[1,64,256]{2,1,0:T(8,128)(2,1)}, f32[1,2,256]{2,1,0:T(2,128)}) custom-call(s32[8]{0:T(128)} %bitcast.3, s32[8]{0:T(128)} %row_offset.1, bf16[8,1024,256]{2,1,0:T(8,128)(2,1)} %modes_hbm.1, bf16[8,1024,256]{2,1,0:T(8,128)(2,1)} %coupling_hbm.1, f32[8,128]{1,0:T(8,128)} %eigenvalues_hbm.1, bf16[1,64,512]{2,1,0:T(8,128)(2,1)} %bitcast.2, ...), custom_call_target="tpu_custom_call" | custom-call | tf_op jit(solution)/shard_map/pallas_call | solution.py:306
  35.6 1.4 %copy.12 = bf16[1,64,256]{2,1,0:T(8,128)(2,1)} copy(bf16[1,64,256]{2,1,0:T(8,128)(2,1)} %get-tuple-element.4) | data formatting | bytes 65536
  37.0 1.2 %copy.13 = f32[1,2,256]{2,1,0:T(2,128)} copy(f32[1,2,256]{2,1,0:T(2,128)} %get-tuple-element.5) | data formatting | bytes 4096

commit v4 on v3

--- a/solution.py
+++ b/solution.py
@@ -143,12 +143,20 @@
     for k in range(2):
         scales[:, k * half:(k + 1) * half] = 1.0 / jnp.sqrt(eigen_both[k])
     slot_copies = {}
-    for d, owner, given, kept in slots:
+    part_copies = {}
+
+    def give(d, owner, given, kept):
         part_send[d] = contract(coupling[given], modes[given], 0, 0).astype(BF16)
-        part_copy = remote(part_send.at[d], part_recv.at[d], part_ssem.at[d], part_rsem.at[d], mode=other)
-        part_copy.start()
+        copy = remote(part_send.at[d], part_recv.at[d], part_ssem.at[d], part_rsem.at[d], mode=other)
+        copy.start()
+        part_copies[d] = copy
+
+    give(*slots[0])
+    for step, (d, owner, given, kept) in enumerate(slots):
         product = contract(coupling[kept], modes[kept], 0, 0)
-        part_copy.wait()
+        if step + 1 < len(slots):
+            give(*slots[step + 1])
+        part_copies[d].wait()
         scaled = ((product + part_recv[d].astype(F32)) * scales[pl.ds(kept, 1), :]).astype(BF16)
         square = contract(scaled, scaled, 1, 1).astype(BF16)
         slot_send[d, 0] = square[:tile, :tile]
@@ -169,12 +177,17 @@
     shift = lax.broadcasted_iota(jnp.int32, (rows, iface), 0) - lax.broadcasted_iota(
         jnp.int32, (rows, iface), 1
     )
+    turned_shift = lax.broadcasted_iota(jnp.int32, (iface, rows), 1) - lax.broadcasted_iota(
+        jnp.int32, (iface, rows), 0
+    )
     for d in [0] + order[:-1]:
         blocks, offsets = (slot_send, offset_send) if d == 0 else (slot_recv, offset_recv)
         if d > 0:
             offset_copies[d].wait()
-        place = jnp.where(shift == offsets[d, 0:1, :], 1.0, 0.0).astype(BF16)
-        places[:, d * iface:(d + 1) * iface] = place
+        place = jnp.where(shift == offsets[d, 0:1, :iface], 1.0, 0.0).astype(BF16)
+        places[d * iface:(d + 1) * iface, :] = jnp.where(
+            turned_shift == offsets[d, 0:1, :], 1.0, 0.0
+        ).astype(BF16)
         if d > 0:
             slot_copies[d].wait()
         corner = blocks[d, 1]
@@ -190,7 +203,7 @@
     pair_rows = 2 * own
     for d, peer in enumerate(peers):
         chunk = placed[pl.ds(pl.multiple_of(peer * pair_rows, pair_rows), pair_rows), :]
-        product = contract(chunk, places[...], 1, 1).reshape(2, own, rows)
+        product = jnp.dot(chunk, places[...], preferred_element_type=F32).reshape(2, own, rows)
         gram[d] = product
         gram_send[d] = product.astype(BF16)
         copy = remote(
@@ -279,10 +292,10 @@
         pltpu.VMEM((leaves, width), F32),
         pltpu.VMEM((ns, 3, iface // 2, iface // 2), BF16),
         pltpu.VMEM((ns, 3, iface // 2, iface // 2), BF16),
-        pltpu.VMEM((ns, 8, iface), jnp.int32),
-        pltpu.VMEM((ns, 8, iface), jnp.int32),
+        pltpu.VMEM((ns, 8, rows), jnp.int32),
+        pltpu.VMEM((ns, 8, rows), jnp.int32),
         pltpu.VMEM((rows, ns * iface), BF16),
-        pltpu.VMEM((rows, ns * iface), BF16),
+        pltpu.VMEM((ns * iface, rows), BF16),
         pltpu.VMEM((nl, nm, own, rows), F32),
         pltpu.VMEM((nl, nm, own, rows), BF16),
         pltpu.VMEM((nl, own, rows), BF16),

time: 38.4 us -> 37.9 us (0.987)
  Pallas kernels: 34.9 us -> 34.4 us
    pallas_call x1, Pallas kernels: 34.9 us -> 34.4 us  [per_device(): pl.pallas_call(functools.partial(kernel, nl, ns), out_shape=(jax.ShapeDty...]
where the time goes in v4:
time: 37.9 us; the launch traced here: 37.7 us
  Pallas kernels  34.4 us (91%)
  local copies, waits for them, and re-layouts  2.62 us (7%)
  between operations  0.64 us (2%)
    pallas_call x1, Pallas kernels, per_device(): pl.pallas_call(functools.partial(kernel, nl, ns), out_shape=(jax.ShapeDty...  34.4 us
    unnamed x2, local copies, waits for them, and re-layouts  2.62 us

profile of v4, /device:TPU:0, one launch (start us, length us, event | category | flops | bytes accessed | tf_op | source)
XLA Modules:
  0.0 37.7 jit_solution(5479113900150875409)
XLA Ops:
  0.6 34.4 %shard_map.95 = (bf16[1,64,256]{2,1,0:T(8,128)(2,1)}, f32[1,2,256]{2,1,0:T(2,128)}) custom-call(s32[8]{0:T(128)} %bitcast.3, s32[8]{0:T(128)} %row_offset.1, bf16[8,1024,256]{2,1,0:T(8,128)(2,1)} %modes_hbm.1, bf16[8,1024,256]{2,1,0:T(8,128)(2,1)} %coupling_hbm.1, f32[8,128]{1,0:T(8,128)} %eigenvalues_hbm.1, bf16[1,64,512]{2,1,0:T(8,128)(2,1)} %bitcast.2, ...), custom_call_target="tpu_custom_call" | custom-call | tf_op jit(solution)/shard_map/pallas_call | solution.py:319
  35.0 1.4 %copy.12 = bf16[1,64,256]{2,1,0:T(8,128)(2,1)} copy(bf16[1,64,256]{2,1,0:T(8,128)(2,1)} %get-tuple-element.4) | data formatting | bytes 65536
  36.4 1.2 %copy.13 = f32[1,2,256]{2,1,0:T(2,128)} copy(f32[1,2,256]{2,1,0:T(2,128)} %get-tuple-element.5) | data formatting | bytes 4096

commit v5 on v4

--- a/solution.py
+++ b/solution.py
@@ -254,16 +254,15 @@
     steps = rotations.shape[1]
     for k in range(steps):
         result = jnp.dot(turned, current, preferred_element_type=F32)
-        column_scale = jnp.sqrt(jnp.sum(result * result, 0, keepdims=True) / rows + EPSILON)
-        norms[0, k:k + 1, :] = column_scale
+        square_sums = jnp.sum(result * result, 0, keepdims=True)
+        norms[0, k:k + 1, :] = square_sums
+        column_scale = jnp.sqrt(square_sums / rows + EPSILON)
         normed = (result * (1.0 / column_scale)).astype(BF16)
         if k < steps - 1:
             current = jnp.dot(normed, rotations[0, k], preferred_element_type=F32).astype(BF16)
         else:
             normed_rows[...] = normed.reshape(normed_rows.shape)
-            out[0] = jnp.dot(
-                normed_rows[leaf, core], rotations[0, k], preferred_element_type=F32
-            ).astype(BF16)
+            out[0] = normed_rows[leaf, core]
 
 
 def per_device(nl, ns, nm, modes, coupling, eigenvalues, separator_of, row_offset, stiffness, start_block, rotations):
@@ -316,7 +315,7 @@
         dma((nl + 1,)), dma((nl + 1,)),
         dma, dma,
     ]
-    return pl.pallas_call(
+    normed, square_sums = pl.pallas_call(
         functools.partial(kernel, nl, ns),
         out_shape=(
             jax.ShapeDtypeStruct((1, own, cols), BF16),
@@ -332,6 +331,8 @@
         separator_of.reshape(leaves), row_offset, modes, coupling, eigenvalues,
         jnp.swapaxes(stiffness, 1, 2), start_block, rotations,
     )
+    subspace = jnp.dot(normed[0], rotations[0, steps - 1], preferred_element_type=F32)
+    return subspace.astype(BF16)[None], jnp.sqrt(square_sums / rows + EPSILON)
 
 
 def solution(mesh):

time: 37.9 us -> 38 us (level)
  local copies, waits for them, and re-layouts: 2.62 us -> 0.01 us
  matrix products: 0 us -> 1.53 us
  other arithmetic: 0 us -> 1.24 us
    unnamed x2, local copies, waits for them, and re-layouts: 2.62 us -> 0.01 us
    dot_general x0 -> x1, matrix products: none -> 1.53 us  [per_device(): jnp.dot(normed[0], rotations[0, steps - 1], preferred_element_type=F32)]
    sqrt x0 -> x1, other arithmetic: none -> 1.24 us  [per_device(): return (subspace.astype(BF16)[None], jnp.sqrt(square_sums / rows + EPSILON))]
where the time goes in v5:
time: 38 us; the launch traced here: 37.8 us
  Pallas kernels  34.3 us (90%)
  matrix products  1.53 us (4%)
  other arithmetic  1.24 us (3%)
  between operations  0.66 us (2%)
    pallas_call x1, Pallas kernels, per_device(): pl.pallas_call(functools.partial(kernel, nl, ns), out_shape=(jax.ShapeDty...  34.3 us
    dot_general x1, matrix products, per_device(): jnp.dot(normed[0], rotations[0, steps - 1], preferred_element_type=F32)  1.53 us
    sqrt x1, other arithmetic, per_device(): return (subspace.astype(BF16)[None], jnp.sqrt(square_sums / rows + EPSILON))  1.24 us

profile of v5, /device:TPU:0, one launch (start us, length us, event | category | flops | bytes accessed | tf_op | source)
XLA Modules:
  0.0 37.8 jit_solution(15718777909017793826)
XLA Ops:
  0.6 0.0 copy-start
  0.6 34.3 %shard_map.95 = (bf16[1,64,256]{2,1,0:T(8,128)(2,1)}, f32[1,2,256]{2,1,0:T(2,128)}) custom-call(s32[8]{0:T(128)} %bitcast.11, s32[8]{0:T(128)} %row_offset.1, bf16[8,1024,256]{2,1,0:T(8,128)(2,1)} %modes_hbm.1, bf16[8,1024,256]{2,1,0:T(8,128)(2,1)} %coupling_hbm.1, f32[8,128]{1,0:T(8,128)} %eigenvalues_hbm.1, bf16[1,64,512]{2,1,0:T(8,128)(2,1)} %bitcast.10, ...), custom_call_target="tpu_custom_call" | custom-call | tf_op jit(solution)/shard_map/pallas_call | solution.py:318
  35.0 0.0 copy-done
  35.0 1.5 %fusion = bf16[1,64,256]{2,1,0:T(8,128)(2,1)} fusion(bf16[1,2,256,256]{3,2,1,0:T(8,128)(2,1)S(1)} %copy-done, bf16[1,64,256]{2,1,0:T(8,128)(2,1)} %get-tuple-element.4), kind=kOutput, calls=%fused_computation.1 | convolution fusion | flops 8404992 | bytes 196608 | tf_op jit(solution)/shard_map/dot_general | solution.py:334
  36.5 1.2 %add_sqrt_fusion = f32[1,2,256]{2,1,0:T(2,128)} fusion(f32[1,2,256]{2,1,0:T(2,128)} %get-tuple-element.5), kind=kLoop, calls=%fused_computation.5 | loop fusion | flops 1024 | bytes 4096 | tf_op jit(solution)/shard_map/sqrt | solution.py:335
Async XLA Ops:
  0.6 34.3 %copy-start = (bf16[1,2,256,256]{3,2,1,0:T(8,128)(2,1)S(1)}, bf16[1,2,256,256]{3,2,1,0:T(8,128)(2,1)}, u32[]{:S(2)}) copy-start(bf16[1,2,256,256]{3,2,1,0:T(8,128)(2,1)} %rotations_hbm.1) | copy-start | bytes 786436

commit v6 on v4

--- a/solution.py
+++ b/solution.py
@@ -61,6 +61,17 @@
     rows = placed.shape[0]
     own, cols = start_block.shape[1:]
 
+    barrier = pltpu.get_barrier_semaphore()
+    pl.semaphore_signal(barrier, inc=1, device_id={"mode": other}, device_id_type=MESH)
+    for d in range(1, ns):
+        pl.semaphore_signal(
+            barrier, inc=1, device_id={"sep": partner(sep, d, ns)}, device_id_type=MESH
+        )
+    for d in range(1, nl):
+        pl.semaphore_signal(
+            barrier, inc=1, device_id={"leaf": lax.rem(leaf + d, nl)}, device_id_type=MESH
+        )
+
     smalls = []
     for k, (src, dst) in enumerate((
         (separator_of, targets), (row_offset, starts), (start_hbm, start_block),
@@ -70,22 +81,14 @@
         copy.start()
         smalls.append(copy)
     loads = []
-    for l in range(leaves):
+    step = leaves // 2
+    for l in range(2):
         for k, (src, dst) in enumerate(((modes_hbm, modes), (coupling_hbm, coupling))):
-            copy = pltpu.make_async_copy(src.at[l], dst.at[l], hbm_sem.at[k, l])
+            part = pl.ds(l * step, step)
+            copy = pltpu.make_async_copy(src.at[part], dst.at[part], hbm_sem.at[k, l])
             copy.start()
             loads.append(copy)
 
-    barrier = pltpu.get_barrier_semaphore()
-    pl.semaphore_signal(barrier, inc=1, device_id={"mode": other}, device_id_type=MESH)
-    for d in range(1, ns):
-        pl.semaphore_signal(
-            barrier, inc=1, device_id={"sep": partner(sep, d, ns)}, device_id_type=MESH
-        )
-    for d in range(1, nl):
-        pl.semaphore_signal(
-            barrier, inc=1, device_id={"leaf": lax.rem(leaf + d, nl)}, device_id_type=MESH
-        )
     smalls[0].wait()
     smalls[1].wait()
 
@@ -305,7 +308,7 @@
         pltpu.VMEM((nl, nm, own, cols), BF16),
         pltpu.VMEM((nl, nm, own, cols), BF16),
         dma((6,)),
-        dma((2, leaves)),
+        dma((2, 2)),
         dma((ns,)), dma((ns,)),
         dma((nl,)), dma((nl,)),
         dma((ns,)), dma((ns,)),

time: 37.9 us -> 37.7 us (level)
  no operation moved by 1% of the time
where the time goes in v6:
time: 37.7 us; the launch traced here: 37.5 us
  Pallas kernels  34.2 us (91%)
  local copies, waits for them, and re-layouts  2.62 us (7%)
  between operations  0.64 us (2%)
    pallas_call x1, Pallas kernels, per_device(): pl.pallas_call(functools.partial(kernel, nl, ns), out_shape=(jax.ShapeDty...  34.2 us
    unnamed x2, local copies, waits for them, and re-layouts  2.62 us

profile of v6, /device:TPU:0, one launch (start us, length us, event | category | flops | bytes accessed | tf_op | source)
XLA Modules:
  0.0 37.5 jit_solution(7936700330441077307)
XLA Ops:
  0.6 34.2 %shard_map.95 = (bf16[1,64,256]{2,1,0:T(8,128)(2,1)}, f32[1,2,256]{2,1,0:T(2,128)}) custom-call(s32[8]{0:T(128)} %bitcast.3, s32[8]{0:T(128)} %row_offset.1, bf16[8,1024,256]{2,1,0:T(8,128)(2,1)} %modes_hbm.1, bf16[8,1024,256]{2,1,0:T(8,128)(2,1)} %coupling_hbm.1, f32[8,128]{1,0:T(8,128)} %eigenvalues_hbm.1, bf16[1,64,512]{2,1,0:T(8,128)(2,1)} %bitcast.2, ...), custom_call_target="tpu_custom_call" | custom-call | tf_op jit(solution)/shard_map/pallas_call | solution.py:322
  34.9 1.4 %copy.12 = bf16[1,64,256]{2,1,0:T(8,128)(2,1)} copy(bf16[1,64,256]{2,1,0:T(8,128)(2,1)} %get-tuple-element.4) | data formatting | bytes 65536
  36.3 1.2 %copy.13 = f32[1,2,256]{2,1,0:T(2,128)} copy(f32[1,2,256]{2,1,0:T(2,128)} %get-tuple-element.5) | data formatting | bytes 4096
